TPU v7x, 256 devices: a whole 4x4x8 slice. The times are simulated.
256 devices in a mesh: dp: 4 (over y), tensor: 16 (over z, x_hi), query: 4 (over x_lo, core).
Axes of the slice: x: 4 (x_hi: 2, x_lo: 2; x = x_hi * 2 + x_lo), y: 4, z: 8, core: 2. Of those that a mesh axis runs over, the one named last changes fastest.
Arguments:
- activations: bfloat16 [64, 512, 28672], P(('dp', 'query'), None, 'tensor'), may hold values from -6 to 6
- out_grads: bfloat16 [64, 512, 8192], P(('dp', 'query'), None, 'tensor'), may hold values from -6 to 6
- token_mask: int32 [64, 512], P(('dp', 'query')), may hold values 0 or 1
- in_proj: bfloat16 [28672, 64], P('tensor'), may hold values from -0.03125 to 0.03125
- out_proj: bfloat16 [8192, 64], P('tensor'), may hold values from -0.0625 to 0.0625
- output_inverse_factor: float32 [64, 64], replicated, may hold values from -0.6 to 3.6, as said below
- input_inverse_factor: float32 [64, 64], replicated, may hold values from -0.6 to 3.6, as said below
- query_grads: float32 [32, 16, 4096], P('query', 'dp', 'tensor'), may hold values from -2 to 2
Outputs:
- scores: float32 [64, 32, 16], P(('dp', 'query'), None, 'tensor')
Inputs may be any that keep to these rules, and one draw needn't show every extreme that they name: `output_inverse_factor`: each factor is its diagonal, between 1 and 3, plus entries of at most 0.6 in magnitude. `input_inverse_factor`: each factor is its diagonal, between 1 and 3, plus entries of at most 0.6 in magnitude.
All inputs are finite; a program needn't handle non-finite values. No bound on the sum of `token_mask` on one device may be relied on, other than what follows from the above.
Results may differ from a plain program's by a relative error of at most 0.0003.
Values sent between devices are 32-bit elements; how exact they have to be, the bound alone decides.
A program may use at most 64 MiB of HBM per device.

v0:
```python
import functools

import jax
import jax.numpy as jnp
from jax import lax
from jax.experimental import pallas as pl
from jax.experimental.pallas import tpu as pltpu
from jax.sharding import PartitionSpec as P

MESH = pl.DeviceIdType.MESH
F32 = jnp.float32
HIGH = lax.Precision.HIGHEST
ORDER = (4, 1, 3, -1, -3, 2, -2, 0)


def nt(a, b, precision=None):
    return lax.dot_general(
        a, b, (((1,), (1,)), ((), ())), precision=precision, preferred_element_type=F32
    )


def tn(a, b, precision=None):
    return lax.dot_general(
        a, b, (((0,), (0,)), ((), ())), precision=precision, preferred_element_type=F32
    )


def kernel(
    act, grads, mask, w_in, w_out, f_out, f_in, query, out,
    act_v, grads_v, mask_v, w_in_v, w_out_v, f_out_v, f_in_v, query_v,
    f_rows, parts, x_got, near_got, three_got, four_got, two_got,
    q_mine, q_all, q_high, q_low, c_send, c_got,
    load_sem, x_send, x_recv, z_send, z_recv, q_send, q_recv, column_send, column_recv,
    c_send_sem, c_recv_sem, here,
):
    dp = lax.axis_index("dp")
    me = lax.axis_index("tensor")
    qi = lax.axis_index("query")
    z, a = me // 2, lax.rem(me, 2)
    x_lo, core = qi // 2, lax.rem(qi, 2)

    def tensor_peer(k):
        return {"tensor": lax.rem(me + k, 16)}

    def dp_peer(k):
        return {"dp": lax.rem(dp + k, 4)}

    def z_peer(k):
        return {"tensor": lax.rem(z + k + 8, 8) * 2 + a}

    lo_peer = {"query": (1 - x_lo) * 2 + core}
    core_peer = {"query": x_lo * 2 + 1 - core}
    x_peer = {"tensor": z * 2 + 1 - a}

    barrier = pltpu.get_barrier_semaphore()
    peers = [x_peer] + [z_peer(k) for k in (1, -1, 2, -2)] + [lo_peer]
    peers += [dp_peer(k) for k in (1, 2, 3)]
    for peer in peers:
        pl.semaphore_signal(barrier, inc=1, device_id=peer, device_id_type=MESH)


    def load(src, dst, n):
        copy = pltpu.make_async_copy(src, dst, load_sem.at[n])
        copy.start()
        return copy

    load_w_in = load(w_in, w_in_v, 0)
    load_w_out = load(w_out, w_out_v, 1)
    load_rows = []
    for n, k in enumerate(ORDER):
        owner = lax.rem(z + k + 8, 8)
        rows = pl.ds(pl.multiple_of(owner * 256, 256), 256)
        load_rows.append(
            (
                load(act.at[rows], act_v.at[n], 7 + 2 * n),
                load(grads.at[rows], grads_v.at[n], 8 + 2 * n),
            )
        )
        if n == 0:
            load_query = load(query, query_v, 2)
    load_mask = load(mask, mask_v, 3)
    load_f_out = load(f_out, f_out_v, 4)
    load_f_in = load(f_in, f_in_v, 5)

    started = []

    def remote(src, dst, send, recv, peer):
        copy = pltpu.make_async_remote_copy(
            src_ref=src, dst_ref=dst, send_sem=send, recv_sem=recv, device_id=peer, device_id_type=MESH
        )
        copy.start()
        started.append(copy)
        return copy

    def project(k):
        n = ORDER.index(k)
        for copy in load_rows[n]:
            copy.wait()
        p_in = nt(w_in_v[...], act_v[n])
        p_out = nt(w_out_v[...], grads_v[n])
        for half in range(2):
            lanes = slice(128 * half, 128 * half + 128)
            parts[2 * n + half, 0:64, :] = p_in[:, lanes]
            parts[2 * n + half, 64:128, :] = p_out[:, lanes]

    def mine(k):
        return 2 * ORDER.index(k) + a

    def other(k):
        return 2 * ORDER.index(k) + 1 - a

    x_copies = {}

    def send_x(k):
        n = ORDER.index(k)
        x_copies[k] = remote(parts.at[other(k)], x_got.at[n], x_send.at[n], x_recv.at[n], x_peer)

    def add_x(k):
        x_copies[k].wait_recv()
        parts[mine(k)] = parts[mine(k)] + x_got[ORDER.index(k)]

    def send_z(n, src, dst, k):
        return remote(src, dst, z_send.at[n], z_recv.at[n], z_peer(k))

    def column_copy(j, source, owner):
        return pltpu.make_async_remote_copy(
            src_ref=q_mine.at[j], dst_ref=q_all.at[source, x_lo, core],
            send_sem=column_send.at[j], recv_sem=column_recv.at[source],
            device_id={"tensor": owner}, device_id_type=MESH,
        )

    def send_column(j):
        owner = dp * 4 + j

        @pl.when(owner == me)
        def _():
            q_all[me, x_lo, core] = q_mine[j]

        @pl.when(owner != me)
        def _():
            column_copy(j, me, owner).start()

    owns = me // 4 == dp
    my_rows = q_all.at[:, x_lo, core]

    def rows_copy(n, peer):
        return pltpu.make_async_remote_copy(
            src_ref=my_rows, dst_ref=my_rows, send_sem=q_send.at[n], recv_sem=q_recv.at[0],
            device_id=peer, device_id_type=MESH,
        )

    load_w_in.wait()
    load_w_out.wait()
    project(4)
    pl.semaphore_wait(barrier, len(peers) + core)
    send_x(4)

    @pl.when(core == 0)
    def _():
        pl.semaphore_signal(barrier, inc=1, device_id=core_peer, device_id_type=MESH)

    pl.semaphore_signal(here.at[0], inc=1, device_id=x_peer, device_id_type=MESH)
    load_query.wait()
    for j in range(4):
        q_mine[j] = query_v[:, j, :]
    project(1)
    near_up = send_z(0, parts.at[other(1)], near_got.at[0, 1 - a], 1)
    project(3)
    send_x(3)
    pl.semaphore_wait(here.at[0], 1)
    pl.semaphore_signal(here.at[1], inc=1, device_id=z_peer(2), device_id_type=MESH)
    pl.semaphore_signal(here.at[2], inc=1, device_id=z_peer(-2), device_id_type=MESH)
    project(-1)
    near_down = send_z(1, parts.at[other(-1)], near_got.at[1, 1 - a], -1)
    project(-3)
    send_x(-3)
    pl.semaphore_wait(here.at[1], 1)
    pl.semaphore_wait(here.at[2], 1)
    for j in range(4):
        send_column(j)
    add_x(4)
    four_up = send_z(2, parts.at[mine(4), 0:64], four_got.at[0], 2)
    four_down = send_z(3, parts.at[mine(4), 64:128], four_got.at[1], -2)
    project(2)
    send_x(2)
    project(-2)
    send_x(-2)
    project(0)
    near_up.wait_recv()
    near_down.wait_recv()
    parts[other(0)] = parts[other(0)] + near_got[0, 1 - a] + near_got[1, 1 - a]
    send_x(0)
    add_x(3)
    three_up = send_z(4, parts.at[mine(3)], three_got.at[0], 1)
    add_x(-3)
    three_down = send_z(5, parts.at[mine(-3)], three_got.at[1], -1)
    own_up = send_z(8, parts.at[mine(1)], near_got.at[0, a], 1)
    own_down = send_z(9, parts.at[mine(-1)], near_got.at[1, a], -1)

    @pl.when(owns)
    def _():
        for k in range(1, 16):
            source = lax.rem(me + k, 16)
            column_copy(0, source, source).wait_recv()
        for k in (1, 2, 3):
            rows_copy(k, dp_peer(k)).start()

    add_x(2)
    three_up.wait_recv()
    four_up.wait_recv()
    n = mine(2)
    parts[n, 0:64] = parts[n, 0:64] + three_got[0, 0:64] + four_got[0]
    parts[n, 64:128] = parts[n, 64:128] + three_got[0, 64:128]
    two_up = send_z(6, parts.at[n], two_got.at[0], 2)
    add_x(-2)
    three_down.wait_recv()
    four_down.wait_recv()
    n = mine(-2)
    parts[n, 0:64] = parts[n, 0:64] + three_got[1, 0:64]
    parts[n, 64:128] = parts[n, 64:128] + three_got[1, 64:128] + four_got[1]
    two_down = send_z(7, parts.at[n], two_got.at[1], -2)
    own_up.wait_recv()
    own_down.wait_recv()
    total = parts[mine(0)] + near_got[0, a] + near_got[1, a]
    load_mask.wait()
    load_f_out.wait()
    load_f_in.wait()
    for i in range(4):
        f_rows[16 * i : 16 * i + 16, :] = f_out_v[pl.ds(i, 16, stride=4), :]
    weights = jnp.zeros((1, 128), F32)
    for n in range(16):
        piece = mask_v[n // 4 : n // 4 + 1, 128 * (n % 4) : 128 * (n % 4) + 128].astype(F32)
        weights = jnp.where(me == n, piece / 512.0, weights)

    x_copies[0].wait_recv()
    total = total + x_got[ORDER.index(0)]
    two_up.wait_recv()
    total = total + two_got[0]
    two_down.wait_recv()
    total = total + two_got[1]

    side_out = jnp.dot(f_rows[...], total[64:128] * weights, precision=HIGH, preferred_element_type=F32)
    side_in = tn(f_in_v[...], total[0:64], HIGH)
    conditioned = nt(side_out, side_in, HIGH)

    for i in range(4):
        c_send[:, 64 * i : 64 * i + 64] = conditioned[16 * i : 16 * i + 16]
    far_first = sorted(range(1, 16), key=lambda k: -min(k // 2, 8 - k // 2))
    c_copies = [
        remote(c_send, c_got.at[me], c_send_sem.at[k - 1], c_recv_sem.at[k - 1], tensor_peer(k))
        for k in far_first
    ]
    c_got[me] = c_send[...]


    @pl.when(jnp.logical_not(owns))
    def _():
        rows_copy(1, dp_peer(1)).wait_recv()

    lo_copy = remote(my_rows, my_rows, q_send.at[4], q_recv.at[1], lo_peer)
    lo_copy.wait_recv()
    block = q_all.at[:, :, core]
    core_copy = pltpu.make_async_remote_copy(
        src_ref=block, dst_ref=block, send_sem=q_send.at[5], recv_sem=q_recv.at[2],
        device_id=core_peer, device_id_type=MESH,
    )
    started.append(core_copy)

    @pl.when(core == 1)
    def _():
        core_copy.start()

    core_copy.wait_recv()

    @pl.when(core == 0)
    def _():
        core_copy.start()

    q = q_all[...].reshape(512, 256)
    high = q.astype(jnp.bfloat16)
    q_high[...] = high
    q_low[...] = (q - high.astype(F32)).astype(jnp.bfloat16)

    for j in range(4):

        @pl.when(dp * 4 + j != me)
        def _():
            column_copy(j, me, dp * 4 + j).wait_send()

    @pl.when(owns)
    def _():
        for k in (1, 2, 3):
            rows_copy(k, dp_peer(k)).wait_send()

    for copy in started:
        copy.wait_send()

    for copy in c_copies[::-1]:
        copy.wait_recv()
    got = c_got[...].reshape(4, 4, 16, 256)
    got = (got[:, 0] + got[:, 1] + got[:, 2] + got[:, 3]).reshape(64, 256)
    high = got.astype(jnp.bfloat16)
    low = (got - high.astype(F32)).astype(jnp.bfloat16)
    pairs = nt(high, q_high[...]) + (nt(high, q_low[...]) + nt(low, q_high[...]))
    left = lax.rem(lax.broadcasted_iota(jnp.int32, (64, 512), 0), 16)
    right = lax.broadcasted_iota(jnp.int32, (64, 512), 1) // 32
    pairs = jnp.where(left == right, pairs, 0.0).reshape(4, 16, 512)
    scores = jnp.sum(pairs, axis=1)
    scores = scores[:, 0:128] + scores[:, 128:256] + scores[:, 256:384] + scores[:, 384:512]
    out[...] = scores[:, 0:32] + scores[:, 32:64] + scores[:, 64:96] + scores[:, 96:128]


def local(act, grads, mask, w_in, w_out, f_out, f_in, query):
    docs, length, hidden = act.shape
    model = grads.shape[2]
    vmem, sem = pltpu.VMEM, pltpu.SemaphoreType.DMA
    scores = pl.pallas_call(
        kernel,
        name="influence",
        out_shape=jax.ShapeDtypeStruct((4, 32), F32),
        in_specs=[pl.BlockSpec(memory_space=pl.ANY)] * 8,
        out_specs=pl.BlockSpec(memory_space=pltpu.VMEM),
        scratch_shapes=[
            vmem((8, 256, hidden), jnp.bfloat16),
            vmem((8, 256, model), jnp.bfloat16),
            vmem((4, 512), jnp.int32),
            vmem((64, hidden), jnp.bfloat16),
            vmem((64, model), jnp.bfloat16),
            vmem((64, 64), F32),
            vmem((64, 64), F32),
            vmem((8, 4, 256), F32),
            vmem((64, 64), F32),
            vmem((16, 128, 128), F32),
            vmem((8, 128, 128), F32),
            vmem((2, 2, 128, 128), F32),
            vmem((2, 128, 128), F32),
            vmem((2, 64, 128), F32),
            vmem((2, 128, 128), F32),
            vmem((4, 8, 256), F32),
            vmem((16, 2, 2, 8, 256), F32),
            vmem((512, 256), jnp.bfloat16),
            vmem((512, 256), jnp.bfloat16),
            vmem((16, 256), F32),
            vmem((16, 16, 256), F32),
            sem((23,)),
            sem((8,)), sem((8,)),
            sem((10,)), sem((10,)),
            sem((6,)), sem((3,)),
            sem((4,)), sem((16,)),
            sem((15,)), sem((15,)),
            pltpu.SemaphoreType.REGULAR((3,)),
        ],
        compiler_params=pltpu.CompilerParams(
            collective_id=0, has_side_effects=True, vmem_limit_bytes=56549376
        ),
    )(
        act.reshape(docs * length, hidden),
        grads.reshape(docs * length, model),
        mask, w_in.T, w_out.T, f_out, f_in, query,
    )
    return scores.reshape(4, 32, 1)


def solution(mesh):
    placed = (
        P(("dp", "query"), None, "tensor"),
        P(("dp", "query"), None, "tensor"),
        P(("dp", "query"), None),
        P("tensor", None),
        P("tensor", None),
        P(),
        P(),
        P("query", "dp", "tensor"),
    )
    return jax.shard_map(
        local,
        mesh=mesh,
        in_specs=placed,
        out_specs=P(("dp", "query"), None, "tensor"),
        check_vma=False,
    )
```

profile of v0, /device:TPU:32, one launch (start us, length us, event | category | flops | bytes accessed | tf_op | source)
XLA Modules:
  0.0 34.5 jit_solution(2908016455778131998)
XLA Ops:
  0.0 33.9 %influence.1 = f32[4,32]{1,0:T(4,128)S(1)} custom-call(bf16[2048,1792]{1,0:T(8,128)(2,1)} %bitcast.8, bf16[2048,512]{1,0:T(8,128)(2,1)} %bitcast.9, s32[4,512]{1,0:T(4,128)} %mask.1, bf16[64,1792]{1,0:T(8,128)(2,1)} %bitcast.10, bf16[64,512]{1,0:T(8,128)(2,1)} %bitcast.11, f32[64,64]{1,0:T(8,128)} %f_out.1, f32[64,64]{1,0:T(8,128)} %f_in.1, f32[8,4,256]{2,1,0:T(4,128)} %query.1), custom_call_target="tpu_custom_call" | custom-call | tf_op jit(solution)/shard_map/influence/pallas_call | solution.py:317
  34.0 0.6 %copy.11 = f32[4,32,1]{1,2,0:T(1,128)} copy(f32[4,32,1]{1,2,0:T(1,128)S(1)} %bitcast.7) | data formatting | bytes 1024
where the time goes:
time: 34.6 us; the launch traced here: 34.5 us
  Pallas kernels  33.9 us (98%)
  local copies, waits for them, and re-layouts  0.58 us (2%)
    pallas_call x1, Pallas kernels, local(): pl.pallas_call(kernel, name='influence', out_shape=jax.ShapeDtypeStruct((...  33.9 us

commit v1 on v0

--- a/solution.py
+++ b/solution.py
@@ -39,9 +39,6 @@
     z, a = me // 2, lax.rem(me, 2)
     x_lo, core = qi // 2, lax.rem(qi, 2)
 
-    def tensor_peer(k):
-        return {"tensor": lax.rem(me + k, 16)}
-
     def dp_peer(k):
         return {"dp": lax.rem(dp + k, 4)}
 
@@ -53,15 +50,15 @@
     x_peer = {"tensor": z * 2 + 1 - a}
 
     barrier = pltpu.get_barrier_semaphore()
-    peers = [x_peer] + [z_peer(k) for k in (1, -1, 2, -2)] + [lo_peer]
-    peers += [dp_peer(k) for k in (1, 2, 3)]
+    peers = [x_peer] + [z_peer(k) for k in (2, -2)] + [dp_peer(k) for k in (2, 1, 3)]
+    peers += [z_peer(k) for k in (1, -1)] + [lo_peer]
     for peer in peers:
         pl.semaphore_signal(barrier, inc=1, device_id=peer, device_id_type=MESH)
 
 
     def load(src, dst, n):
         copy = pltpu.make_async_copy(src, dst, load_sem.at[n])
-        copy.start()
+        copy.start(priority=1)
         return copy
 
     load_w_in = load(w_in, w_in_v, 0)
@@ -245,11 +242,11 @@
 
     for i in range(4):
         c_send[:, 64 * i : 64 * i + 64] = conditioned[16 * i : 16 * i + 16]
-    far_first = sorted(range(1, 16), key=lambda k: -min(k // 2, 8 - k // 2))
-    c_copies = [
-        remote(c_send, c_got.at[me], c_send_sem.at[k - 1], c_recv_sem.at[k - 1], tensor_peer(k))
-        for k in far_first
-    ]
+    far_first = [(k, row) for k in (4, 3, -3, 2, -2, 1, -1, 0) for row in (0, 1) if (k, row) != (0, 0)]
+    c_copies = []
+    for n, (k, row) in enumerate(far_first):
+        peer = lax.rem(z + k + 8, 8) * 2 + (1 - a if row else a)
+        c_copies.append(remote(c_send, c_got.at[me], c_send_sem.at[n], c_recv_sem.at[n], {"tensor": peer}))
     c_got[me] = c_send[...]
 
 

time: 34.6 us -> 34.5 us (level)
  no operation moved by 1% of the time
where the time goes in v1:
time: 34.5 us; the launch traced here: 34.3 us
  Pallas kernels  33.8 us (98%)
  local copies, waits for them, and re-layouts  0.58 us (2%)
    pallas_call x1, Pallas kernels, local(): pl.pallas_call(kernel, name='influence', out_shape=jax.ShapeDtypeStruct((...  33.8 us

profile of v1, /device:TPU:32, one launch (start us, length us, event | category | flops | bytes accessed | tf_op | source)
XLA Modules:
  0.0 34.3 jit_solution(1916765797727788173)
XLA Ops:
  0.0 33.8 %influence.1 = f32[4,32]{1,0:T(4,128)S(1)} custom-call(bf16[2048,1792]{1,0:T(8,128)(2,1)} %bitcast.8, bf16[2048,512]{1,0:T(8,128)(2,1)} %bitcast.9, s32[4,512]{1,0:T(4,128)} %mask.1, bf16[64,1792]{1,0:T(8,128)(2,1)} %bitcast.10, bf16[64,512]{1,0:T(8,128)(2,1)} %bitcast.11, f32[64,64]{1,0:T(8,128)} %f_out.1, f32[64,64]{1,0:T(8,128)} %f_in.1, f32[8,4,256]{2,1,0:T(4,128)} %query.1), custom_call_target="tpu_custom_call" | custom-call | tf_op jit(solution)/shard_map/influence/pallas_call | solution.py:314
  33.8 0.6 %copy.11 = f32[4,32,1]{1,2,0:T(1,128)} copy(f32[4,32,1]{1,2,0:T(1,128)S(1)} %bitcast.7) | data formatting | bytes 1024

commit v2 on v1

--- a/solution.py
+++ b/solution.py
@@ -222,8 +222,9 @@
     load_mask.wait()
     load_f_out.wait()
     load_f_in.wait()
+    f_blocks = f_out_v[...].reshape(16, 4, 64)
     for i in range(4):
-        f_rows[16 * i : 16 * i + 16, :] = f_out_v[pl.ds(i, 16, stride=4), :]
+        f_rows[16 * i : 16 * i + 16, :] = f_blocks[:, i, :]
     weights = jnp.zeros((1, 128), F32)
     for n in range(16):
         piece = mask_v[n // 4 : n // 4 + 1, 128 * (n % 4) : 128 * (n % 4) + 128].astype(F32)

time: 34.5 us -> 34.5 us (level)
  no operation moved by 1% of the time
where the time goes in v2:
time: 34.5 us; the launch traced here: 34.3 us
  Pallas kernels  33.8 us (98%)
  local copies, waits for them, and re-layouts  0.58 us (2%)
    pallas_call x1, Pallas kernels, local(): pl.pallas_call(kernel, name='influence', out_shape=jax.ShapeDtypeStruct((...  33.8 us

profile of v2, /device:TPU:32, one launch (start us, length us, event | category | flops | bytes accessed | tf_op | source)
XLA Modules:
  0.0 34.3 jit_solution(13395660926177558033)
XLA Ops:
  0.0 33.8 %influence.1 = f32[4,32]{1,0:T(4,128)S(1)} custom-call(bf16[2048,1792]{1,0:T(8,128)(2,1)} %bitcast.8, bf16[2048,512]{1,0:T(8,128)(2,1)} %bitcast.9, s32[4,512]{1,0:T(4,128)} %mask.1, bf16[64,1792]{1,0:T(8,128)(2,1)} %bitcast.10, bf16[64,512]{1,0:T(8,128)(2,1)} %bitcast.11, f32[64,64]{1,0:T(8,128)} %f_out.1, f32[64,64]{1,0:T(8,128)} %f_in.1, f32[8,4,256]{2,1,0:T(4,128)} %query.1), custom_call_target="tpu_custom_call" | custom-call | tf_op jit(solution)/shard_map/influence/pallas_call | solution.py:315
  33.8 0.6 %copy.11 = f32[4,32,1]{1,2,0:T(1,128)} copy(f32[4,32,1]{1,2,0:T(1,128)S(1)} %bitcast.7) | data formatting | bytes 1024

commit v3 on v2

--- a/solution.py
+++ b/solution.py
@@ -9,7 +9,6 @@
 
 MESH = pl.DeviceIdType.MESH
 F32 = jnp.float32
-HIGH = lax.Precision.HIGHEST
 ORDER = (4, 1, 3, -1, -3, 2, -2, 0)
 
 
@@ -23,6 +22,13 @@
     return lax.dot_general(
         a, b, (((0,), (0,)), ((), ())), precision=precision, preferred_element_type=F32
     )
+
+
+def three(product, p, q):
+    p_high, q_high = p.astype(jnp.bfloat16), q.astype(jnp.bfloat16)
+    p_low = (p - p_high.astype(F32)).astype(jnp.bfloat16)
+    q_low = (q - q_high.astype(F32)).astype(jnp.bfloat16)
+    return product(p_high, q_high) + (product(p_high, q_low) + product(p_low, q_high))
 
 
 def kernel(
@@ -237,9 +243,9 @@
     two_down.wait_recv()
     total = total + two_got[1]
 
-    side_out = jnp.dot(f_rows[...], total[64:128] * weights, precision=HIGH, preferred_element_type=F32)
-    side_in = tn(f_in_v[...], total[0:64], HIGH)
-    conditioned = nt(side_out, side_in, HIGH)
+    side_out = three(lambda p, q: jnp.dot(p, q, preferred_element_type=F32), f_rows[...], total[64:128] * weights)
+    side_in = three(tn, f_in_v[...], total[0:64])
+    conditioned = three(nt, side_out, side_in)
 
     for i in range(4):
         c_send[:, 64 * i : 64 * i + 64] = conditioned[16 * i : 16 * i + 16]

time: 34.5 us -> 34.2 us (level)
  no operation moved by 1% of the time
where the time goes in v3:
time: 34.2 us; the launch traced here: 34.1 us
  Pallas kernels  33.5 us (98%)
  local copies, waits for them, and re-layouts  0.58 us (2%)
    pallas_call x1, Pallas kernels, local(): pl.pallas_call(kernel, name='influence', out_shape=jax.ShapeDtypeStruct((...  33.5 us

profile of v3, /device:TPU:32, one launch (start us, length us, event | category | flops | bytes accessed | tf_op | source)
XLA Modules:
  0.0 34.1 jit_solution(2352206906139339013)
XLA Ops:
  0.0 33.5 %influence.1 = f32[4,32]{1,0:T(4,128)S(1)} custom-call(bf16[2048,1792]{1,0:T(8,128)(2,1)} %bitcast.8, bf16[2048,512]{1,0:T(8,128)(2,1)} %bitcast.9, s32[4,512]{1,0:T(4,128)} %mask.1, bf16[64,1792]{1,0:T(8,128)(2,1)} %bitcast.10, bf16[64,512]{1,0:T(8,128)(2,1)} %bitcast.11, f32[64,64]{1,0:T(8,128)} %f_out.1, f32[64,64]{1,0:T(8,128)} %f_in.1, f32[8,4,256]{2,1,0:T(4,128)} %query.1), custom_call_target="tpu_custom_call" | custom-call | tf_op jit(solution)/shard_map/influence/pallas_call | solution.py:321
  33.5 0.6 %copy.11 = f32[4,32,1]{1,2,0:T(1,128)} copy(f32[4,32,1]{1,2,0:T(1,128)S(1)} %bitcast.7) | data formatting | bytes 1024
